TPU v7x, 32 devices: a whole 2x2x4 slice. The times are simulated.
32 devices in a mesh: groups: 1, dom: 32 (over z, y, x, core).
Axes of the slice: x: 2, y: 2, z: 4, core: 2. Of those that a mesh axis runs over, the one named last changes fastest.
Arguments:
- feats: bfloat16 [32768, 512], P(('groups', 'dom')), may hold values from -6 to 6
- pre_act: bfloat16 [32768, 512], P(('groups', 'dom')), may hold values from -6 to 6
- cotangent: bfloat16 [32768, 512], P(('groups', 'dom')), may hold values from -6 to 6
- w_self1: bfloat16 [512, 512], replicated, may hold values from -0.25 to 0.25
- w_neigh1: bfloat16 [512, 512], replicated, may hold values from -0.25 to 0.25
- w_self2: bfloat16 [512, 512], replicated, may hold values from -0.25 to 0.25
- w_neigh2: bfloat16 [512, 512], replicated, may hold values from -0.25 to 0.25
- local_tiles: bfloat16 [768, 128, 128], P(('groups', 'dom')), may hold values from -0.25 to 0.25
- local_coords: int32 [768, 2], P(('groups', 'dom')), may hold values from 0 to 7
- remote_tiles: bfloat16 [512, 128, 128], P(('groups', 'dom')), may hold values from -0.25 to 0.25
- remote_rows: int32 [512], P(('groups', 'dom')), may hold values from 0 to 7
- remote_slots: int32 [512], P(('groups', 'dom')), may hold values from 0 to 1
- send_rows: int32 [32, 32, 8], P(('groups', 'dom')), may hold values from 0 to 1023
- send_count: int32 [32, 32], P(('groups', 'dom')), may hold values from 0 to 8, as said below
Outputs:
- feat_grad: float32 [32768, 512], P(('groups', 'dom'))
- grad_self1: float32 [512, 512], P('groups')
- grad_neigh1: float32 [512, 512], P('groups')
- grad_self2: float32 [512, 512], P('groups')
- grad_neigh2: float32 [512, 512], P('groups')
Inputs may be any that keep to these rules, and one draw needn't show every extreme that they name: `send_count`: the diagonal is 0, and in every draw some partition receives 8 rows from every other partition.
All inputs are finite; a program needn't handle non-finite values.
Results may differ from a plain program's by a relative error of at most 0.004.
Values may be sent and summed in bfloat16 or wider, within the bound.
A program may use at most 128 MiB of HBM per device.

v0:
```python
import functools

import jax
import jax.numpy as jnp
from jax import lax
from jax.experimental import pallas as pl
from jax.experimental.pallas import tpu as pltpu
from jax.sharding import PartitionSpec as P

F32 = jnp.float32
BF16 = jnp.bfloat16
MESH = pl.DeviceIdType.MESH
VMEM_LIMIT = 52 * 1024 * 1024


def mm(a, b, ca, cb):
    return lax.dot_general(a, b, (((ca,), (cb,)), ((), ())), preferred_element_type=F32)


def dense_kernel(coords, rrows, rslots, ltiles, rtiles, d_out, rt_out, d_acc, rt_acc):
    side = ltiles.shape[1]
    d_acc[...] = jnp.zeros_like(d_acc)
    rt_acc[...] = jnp.zeros_like(rt_acc)

    @pl.loop(0, ltiles.shape[0])
    def _(t):
        r = pl.multiple_of(coords[t, 0] * side, side)
        q = pl.multiple_of(coords[t, 1] * side, side)
        d_acc[pl.ds(q, side), pl.ds(r, side)] += ltiles[t].astype(F32).T

    @pl.loop(0, rtiles.shape[0])
    def _(t):
        r = pl.multiple_of(rrows[t] * side, side)
        q = pl.multiple_of(rslots[t] * side, side)
        rt_acc[pl.ds(q, side), pl.ds(r, side)] += rtiles[t].astype(F32).T

    for acc, out in ((d_acc, d_out), (rt_acc, rt_out)):
        whole = acc[...]
        high = whole.astype(BF16)
        out[0] = high
        out[1] = (whole - high.astype(F32)).astype(BF16)


def main_kernel(
    n,
    feats,
    pre,
    cot,
    ws1,
    wn1,
    ws2,
    wn2,
    dense,
    rt,
    idx,
    fg_out,
    gr_out,
    hid,
    low,
    rest,
    up1,
    onehot,
    acc_s,
    acc_o,
    sb,
    arr,
    part,
    sibr,
    half,
    rsr,
    ag,
    a2a_send,
    a2a_recv,
    sib_send,
    sib_recv,
    rs_send,
    rs_recv,
    ag_send,
    ag_recv,
):
    nl, f = feats.shape
    m = n // 2
    fh = f // 2
    me = lax.axis_index("dom")
    chip = me // 2
    core = me % 2
    sibling = chip * 2 + 1 - core
    blk = 256
    barrier = pltpu.get_barrier_semaphore()

    @pl.loop(1, n)
    def _(k):
        pl.semaphore_signal(
            barrier, inc=1, device_id={"dom": lax.rem(me + k, n)}, device_id_type=MESH
        )

    def a2a_copy(l, k):
        peer = lax.rem(me + k, n)
        return pltpu.make_async_remote_copy(
            src_ref=sb.at[l, peer],
            dst_ref=arr.at[l, me],
            send_sem=a2a_send.at[l, k],
            recv_sem=a2a_recv.at[l, k],
            device_id={"dom": peer},
            device_id_type=MESH,
        )

    def sib_copy(l):
        return pltpu.make_async_remote_copy(
            src_ref=part.at[l, 1 - core],
            dst_ref=sibr.at[l],
            send_sem=sib_send.at[l],
            recv_sem=sib_recv.at[l],
            device_id={"dom": sibling},
            device_id_type=MESH,
        )

    def rs_copy(l, k):
        to = lax.rem(chip + k, m)
        return pltpu.make_async_remote_copy(
            src_ref=half.at[l, to],
            dst_ref=rsr.at[l, chip],
            send_sem=rs_send.at[l, k],
            recv_sem=rs_recv.at[l, k],
            device_id={"dom": to * 2 + core},
            device_id_type=MESH,
        )

    def ag_copy(l, k):
        to = lax.rem(chip + k, m)
        return pltpu.make_async_remote_copy(
            src_ref=ag.at[l, core, chip],
            dst_ref=ag.at[l, core, chip],
            send_sem=ag_send.at[l, k],
            recv_sem=ag_recv.at[l, k],
            device_id={"dom": to * 2 + core},
            device_id_type=MESH,
        )

    def fwd_copy(l):
        return pltpu.make_async_remote_copy(
            src_ref=ag.at[l, core],
            dst_ref=ag.at[l, core],
            send_sem=sib_send.at[2 + l],
            recv_sem=sib_recv.at[2 + l],
            device_id={"dom": sibling},
            device_id_type=MESH,
        )

    def each(count, l, copy, action):
        @pl.loop(1, count)
        def _(k):
            getattr(copy(l, k), action)()

    def slot_back(l, g):
        back = mm(rt[0], g[...], 1, 0) + mm(rt[1], g[...], 1, 0)
        left = back[:, :fh].reshape(n, -1, fh)
        right = back[:, fh:].reshape(n, -1, fh)
        sb[l] = jnp.concatenate([left, right], axis=1).astype(BF16)

    def local_part(g, ws):
        @pl.loop(0, nl // blk)
        def _(i):
            rows = pl.ds(pl.multiple_of(i * blk, blk), blk)
            acc_s[rows, :] = mm(dense[0, rows, :], g[...], 1, 0) + mm(
                dense[1, rows, :], g[...], 1, 0
            )
            acc_o[rows, :] = mm(g[rows, :], ws[...], 1, 1)

    def gradient(l, which, h, *terms):
        for i in range(f // blk):
            cols = slice(i * blk, (i + 1) * blk)
            part[l, which, cols, :] = sum(mm(h[:, cols], g[...], 0, 0) for g in terms)

    def finish(l, wn, emit):
        got = arr[l].astype(F32)
        cap = got.shape[1] // 2
        left = got[:, :cap, :].reshape(n * cap, fh).astype(BF16)
        right = got[:, cap:, :].reshape(n * cap, fh).astype(BF16)
        got = jnp.concatenate([left, right], axis=1)

        @pl.loop(0, nl // blk)
        def _(i):
            rows = pl.ds(pl.multiple_of(i * blk, blk), blk)
            summed = acc_s[rows, :] + mm(onehot[rows, :], got, 1, 0)
            high = summed.astype(BF16)
            low[rows, :] = high
            rest[rows, :] = (summed - high.astype(F32)).astype(BF16)
            emit(rows, acc_o[rows, :] + mm(low[rows, :], wn[...], 1, 1))

    def reduce_start(l):
        sib_copy(l).wait_recv()
        mine = part[l, core] + sibr[l]
        half[l] = mine.astype(BF16).reshape(half.shape[1:])
        each(m, l, rs_copy, "start")

    def reduce_end(l):
        each(m, l, rs_copy, "wait_recv")
        total = half[l, chip].astype(F32)
        for k in range(1, m):
            total = total + rsr[l, lax.rem(chip + k, m)].astype(F32)
        ag[l, core, chip] = total.astype(BF16)
        each(m, l, ag_copy, "start")

    slot_back(0, cot)
    arr[0, me] = jnp.zeros_like(arr[0, me])
    arr[1, me] = jnp.zeros_like(arr[1, me])
    pl.semaphore_wait(barrier, n - 1)
    each(n, 0, a2a_copy, "start")
    hid[...] = jnp.maximum(pre[...], jnp.zeros_like(pre))
    local_part(cot, ws2)
    gradient(0, 0, hid, cot)
    onehot[...] = jnp.where(
        lax.broadcasted_iota(jnp.int32, onehot.shape, 0) == idx[...], 1.0, 0.0
    ).astype(BF16)
    each(n, 0, a2a_copy, "wait_recv")

    def emit_two(rows, value):
        up1[rows, :] = jnp.where(pre[rows, :].astype(F32) > 0, value, 0.0).astype(BF16)

    finish(0, wn2, emit_two)
    slot_back(1, up1)
    each(n, 1, a2a_copy, "start")
    gradient(0, 1, hid, low, rest)
    sib_copy(0).start()
    local_part(up1, ws1)
    reduce_start(0)
    gradient(1, 0, feats, up1)
    each(n, 1, a2a_copy, "wait_recv")

    def emit_one(rows, value):
        fg_out[rows, :] = value

    finish(1, wn1, emit_one)
    gradient(1, 1, feats, low, rest)
    sib_copy(1).start()
    reduce_end(0)
    reduce_start(1)
    reduce_end(1)
    each(m, 0, ag_copy, "wait_recv")
    fwd_copy(0).start()
    each(m, 1, ag_copy, "wait_recv")
    fwd_copy(1).start()
    each(n, 0, a2a_copy, "wait_send")
    each(n, 1, a2a_copy, "wait_send")
    for l in range(2):
        sib_copy(l).wait_send()
        each(m, l, rs_copy, "wait_send")
        each(m, l, ag_copy, "wait_send")
    for l in range(2):
        fwd_copy(l).wait()
        gr_out[l] = ag[l].reshape(gr_out.shape[1:])


def per_device(
    feats,
    pre_act,
    cotangent,
    w_self1,
    w_neigh1,
    w_self2,
    w_neigh2,
    local_tiles,
    local_coords,
    remote_tiles,
    remote_rows,
    remote_slots,
    send_rows,
    send_count,
):
    n = lax.axis_size("dom")
    m = n // 2
    nl, f = feats.shape
    cap = send_rows.shape[2]
    slots = n * cap
    vmem = pl.BlockSpec(memory_space=pltpu.VMEM)
    smem = pl.BlockSpec(memory_space=pltpu.SMEM)
    dense, rt = pl.pallas_call(
        dense_kernel,
        out_shape=(
            jax.ShapeDtypeStruct((2, nl, nl), BF16),
            jax.ShapeDtypeStruct((2, slots, nl), BF16),
        ),
        in_specs=[smem, smem, smem, vmem, vmem],
        out_specs=(vmem, vmem),
        scratch_shapes=[pltpu.VMEM((nl, nl), F32), pltpu.VMEM((slots, nl), F32)],
        compiler_params=pltpu.CompilerParams(vmem_limit_bytes=VMEM_LIMIT),
        name="dense",
    )(local_coords, remote_rows, remote_slots, local_tiles, remote_tiles)

    live = jnp.arange(cap)[None, :] < send_count[0][:, None]
    idx = jnp.where(live, send_rows[0], -1).reshape(1, slots)
    chunk = f // m
    dma = pltpu.SemaphoreType.DMA
    feat_grad, grads = pl.pallas_call(
        functools.partial(main_kernel, n),
        out_shape=(
            jax.ShapeDtypeStruct((nl, f), F32),
            jax.ShapeDtypeStruct((2, 2, f, f), BF16),
        ),
        in_specs=[vmem] * 10,
        out_specs=(vmem, vmem),
        scratch_shapes=[
            pltpu.VMEM((nl, f), BF16),
            pltpu.VMEM((nl, f), BF16),
            pltpu.VMEM((nl, f), BF16),
            pltpu.VMEM((nl, f), BF16),
            pltpu.VMEM((nl, slots), BF16),
            pltpu.VMEM((nl, f), F32),
            pltpu.VMEM((nl, f), F32),
            pltpu.VMEM((2, n, 2 * cap, f // 2), BF16),
            pltpu.VMEM((2, n, 2 * cap, f // 2), BF16),
            pltpu.VMEM((2, 2, f, f), F32),
            pltpu.VMEM((2, f, f), F32),
            pltpu.VMEM((2, m, chunk, f), BF16),
            pltpu.VMEM((2, m, chunk, f), BF16),
            pltpu.VMEM((2, 2, m, chunk, f), BF16),
            dma((2, n)),
            dma((2, n)),
            dma((4,)),
            dma((4,)),
            dma((2, m)),
            dma((2, m)),
            dma((2, m)),
            dma((2, m)),
        ],
        compiler_params=pltpu.CompilerParams(
            collective_id=0, has_side_effects=True, vmem_limit_bytes=VMEM_LIMIT
        ),
        name="main",
    )(
        feats,
        pre_act,
        cotangent,
        w_self1,
        w_neigh1,
        w_self2,
        w_neigh2,
        dense,
        rt,
        idx,
    )
    grads = grads.astype(F32)
    return (feat_grad, grads[1, 0], grads[1, 1], grads[0, 0], grads[0, 1])


def solution(mesh):
    return jax.shard_map(
        per_device,
        mesh=mesh,
        in_specs=(
            P(("groups", "dom"), None),
            P(("groups", "dom"), None),
            P(("groups", "dom"), None),
            P(),
            P(),
            P(),
            P(),
            P(("groups", "dom"), None, None),
            P(("groups", "dom"), None),
            P(("groups", "dom"), None, None),
            P(("groups", "dom")),
            P(("groups", "dom")),
            P(("groups", "dom"), None, None),
            P(("groups", "dom"), None),
        ),
        out_specs=(
            P(("groups", "dom"), None),
            P("groups", None),
            P("groups", None),
            P("groups", None),
            P("groups", None),
        ),
        check_vma=False,
    )
```

profile of v0, /device:TPU:17, one launch (start us, length us, event | category | flops | bytes accessed | tf_op | source)
XLA Modules:
  0.0 107.0 jit_solution(5464862974794387056)
XLA Ops:
  0.6 0.7 iota_compare_fusion
  1.4 0.1 lt.29
  1.5 0.8 copy.21.coords
  2.2 0.8 copy.22
  3.0 0.1 squeeze.15
  3.1 0.0 copy-start
  3.1 1.1 %copy-done = bf16[24,128,128]{2,1,0:T(8,128)(2,1)S(1)} copy-done((bf16[24,128,128]{2,1,0:T(8,128)(2,1)S(1)}, bf16[24,128,128]{2,1,0:T(8,128)(2,1)}, u32[]{:S(2)}) %copy-start) | copy-done | bytes 786456
  4.2 0.0 copy-start.1
  4.2 1.0 copy-done.1
  5.3 0.0 copy-start.5
  5.3 0.7 copy-done.5
  5.9 0.0 copy-start.6
  5.9 0.7 copy-done.6
  6.6 8.2 %dense.1 = (bf16[2,1024,1024]{2,1,0:T(8,128)(2,1)}, bf16[2,256,1024]{2,1,0:T(8,128)(2,1)}) custom-call(s32[24,2]{1,0:T(8,128)S(1)} %copy.21.coords, s32[16]{0:T(128)S(1)} %copy-done.5, s32[16]{0:T(128)S(1)} %copy-done.6, bf16[24,128,128]{2,1,0:T(8,128)(2,1)S(1)} %copy-done, bf16[16,128,128]{2,1,0:T(8,128)(2,1)S(1)} %copy-done.1), custom_call_target="tpu_custom_call" | custom-call | tf_op jit(solution)/shard_map/dense/pallas_call | solution.py:278
  14.7 0.0 copy-start.2
  14.7 1.0 copy-done.2
  15.8 0.0 copy-start.3
  15.8 1.0 copy-done.3
  16.8 0.0 copy-start.4
  16.8 1.0 copy-done.4
  17.9 82.7 %main.1 = (f32[1024,512]{1,0:T(8,128)}, bf16[2,2,512,512]{3,2,1,0:T(8,128)(2,1)}) custom-call(bf16[1024,512]{1,0:T(8,128)(2,1)} %feats.1, bf16[1024,512]{1,0:T(8,128)(2,1)} %pre.1, bf16[1024,512]{1,0:T(8,128)(2,1)} %cot.1, bf16[512,512]{1,0:T(8,128)(2,1)S(1)} %copy-done.2, bf16[512,512]{1,0:T(8,128)(2,1)S(1)} %copy-done.3, bf16[512,512]{1,0:T(8,128)(2,1)S(1)} %copy-done.4, ...), custom_call_target="tpu_custom_call" | custom-call | tf_op jit(solution)/shard_map/main/pallas_call | solution.py:295
  100.6 2.2 %convert_element_type.3 = f32[2,2,512,512]{3,2,1,0:T(8,128)S(1)} convert(bf16[2,2,512,512]{3,2,1,0:T(8,128)(2,1)} %get-tuple-element.12) | non-fusion elementwise | flops 1048576 | bytes 6291456 | tf_op jit(solution)/shard_map/convert_element_type | solution.py:343
  102.8 0.0 copy-start.7
  102.8 2.1 %slice_bitcast_fusion = (f32[512,512]{1,0:T(8,128)}, f32[512,512]{1,0:T(8,128)}, f32[512,512]{1,0:T(8,128)}, f32[512,512]{1,0:T(8,128)}) fusion(f32[2,2,512,512]{3,2,1,0:T(8,128)S(1)} %convert_element_type.3), kind=kLoop, calls=%fused_computation | loop fusion | bytes 8388608 | tf_op jit(solution)/shard_map/squeeze | solution.py:344
  104.9 0.8 copy-done.7
  105.7 1.3 %copy.24 = f32[1024,512]{1,0:T(8,128)} copy(f32[1024,512]{1,0:T(8,128)S(1)} %copy-done.7) | data formatting | bytes 4194304
  (1 shorter events, 0.0 us)
Async XLA Ops:
  3.1 1.1 %copy-start = (bf16[24,128,128]{2,1,0:T(8,128)(2,1)S(1)}, bf16[24,128,128]{2,1,0:T(8,128)(2,1)}, u32[]{:S(2)}) copy-start(bf16[24,128,128]{2,1,0:T(8,128)(2,1)} %ltiles.1) | copy-start | bytes 2359300
  4.2 1.0 copy-start.1
  5.3 0.7 copy-start.5
  5.9 0.7 copy-start.6
  14.7 1.0 copy-start.2
  15.8 1.0 copy-start.3
  16.8 1.0 copy-start.4
  102.8 2.9 %copy-start.7 = (f32[1024,512]{1,0:T(8,128)S(1)}, f32[1024,512]{1,0:T(8,128)}, u32[]{:S(2)}) copy-start(f32[1024,512]{1,0:T(8,128)} %get-tuple-element.22) | copy-start | bytes 6291460
where the time goes:
time: 108 us; the launch traced here: 107 us
  Pallas kernels  90.9 us (84%)
  local copies, waits for them, and re-layouts  12.6 us (12%)
  other arithmetic  2.9 us (3%)
    pallas_call x1, Pallas kernels, per_device(): pl.pallas_call(functools.partial(main_kernel, n), out_shape=(jax.ShapeDty...  82.7 us
    unnamed x19, local copies, waits for them, and re-layouts  10.3 us
    pallas_call x1, Pallas kernels, per_device(): pl.pallas_call(dense_kernel, out_shape=(jax.ShapeDtypeStruct((2, nl, nl),...  8.17 us
    convert_element_type x1, other arithmetic, per_device(): grads = grads.astype(F32)  2.17 us

commit v1 on v0

--- a/solution.py
+++ b/solution.py
@@ -54,7 +54,10 @@
     rt,
     idx,
     fg_out,
-    gr_out,
+    gs1_out,
+    gn1_out,
+    gs2_out,
+    gn2_out,
     hid,
     low,
     rest,
@@ -67,23 +70,31 @@
     part,
     sibr,
     half,
-    rsr,
+    rsp,
+    mid,
+    rsl,
     ag,
     a2a_send,
     a2a_recv,
     sib_send,
     sib_recv,
-    rs_send,
-    rs_recv,
-    ag_send,
-    ag_recv,
+    rp_send,
+    rp_recv,
+    rl_send,
+    rl_recv,
+    al_send,
+    al_recv,
+    ap_send,
+    ap_recv,
 ):
     nl, f = feats.shape
-    m = n // 2
     fh = f // 2
+    plane, layers = half.shape[1:3]
     me = lax.axis_index("dom")
     chip = me // 2
     core = me % 2
+    place = chip % plane
+    layer = chip // plane
     sibling = chip * 2 + 1 - core
     blk = 256
     barrier = pltpu.get_barrier_semaphore()
@@ -115,27 +126,45 @@
             device_id_type=MESH,
         )
 
-    def rs_copy(l, k):
-        to = lax.rem(chip + k, m)
+    def plane_copy(src, dst, send, recv, l, k):
+        to = lax.rem(place + k, plane)
         return pltpu.make_async_remote_copy(
-            src_ref=half.at[l, to],
-            dst_ref=rsr.at[l, chip],
-            send_sem=rs_send.at[l, k],
-            recv_sem=rs_recv.at[l, k],
-            device_id={"dom": to * 2 + core},
+            src_ref=src(to),
+            dst_ref=dst,
+            send_sem=send.at[l, k],
+            recv_sem=recv.at[l, k],
+            device_id={"dom": (layer * plane + to) * 2 + core},
             device_id_type=MESH,
         )
 
-    def ag_copy(l, k):
-        to = lax.rem(chip + k, m)
+    def layer_copy(src, dst, send, recv, l, k):
+        to = lax.rem(layer + k, layers)
         return pltpu.make_async_remote_copy(
-            src_ref=ag.at[l, core, chip],
-            dst_ref=ag.at[l, core, chip],
-            send_sem=ag_send.at[l, k],
-            recv_sem=ag_recv.at[l, k],
-            device_id={"dom": to * 2 + core},
+            src_ref=src(to),
+            dst_ref=dst,
+            send_sem=send.at[l, k],
+            recv_sem=recv.at[l, k],
+            device_id={"dom": (to * plane + place) * 2 + core},
             device_id_type=MESH,
         )
+
+    def rs_plane(l, k):
+        return plane_copy(
+            lambda to: half.at[l, to], rsp.at[l, place], rp_send, rp_recv, l, k
+        )
+
+    def rs_layer(l, k):
+        return layer_copy(
+            lambda to: mid.at[l, to], rsl.at[l, layer], rl_send, rl_recv, l, k
+        )
+
+    def ag_layer(l, k):
+        own = ag.at[l, core, place, layer]
+        return layer_copy(lambda to: own, own, al_send, al_recv, l, k)
+
+    def ag_plane(l, k):
+        own = ag.at[l, core, place]
+        return plane_copy(lambda to: own, own, ap_send, ap_recv, l, k)
 
     def fwd_copy(l):
         return pltpu.make_async_remote_copy(
@@ -192,15 +221,31 @@
         sib_copy(l).wait_recv()
         mine = part[l, core] + sibr[l]
         half[l] = mine.astype(BF16).reshape(half.shape[1:])
-        each(m, l, rs_copy, "start")
+        each(plane, l, rs_plane, "start")
+
+    def reduce_middle(l):
+        each(plane, l, rs_plane, "wait_recv")
+        total = half[l, place].astype(F32)
+        for k in range(1, plane):
+            total = total + rsp[l, lax.rem(place + k, plane)].astype(F32)
+        mid[l] = total.astype(BF16)
+        each(layers, l, rs_layer, "start")
 
     def reduce_end(l):
-        each(m, l, rs_copy, "wait_recv")
-        total = half[l, chip].astype(F32)
-        for k in range(1, m):
-            total = total + rsr[l, lax.rem(chip + k, m)].astype(F32)
-        ag[l, core, chip] = total.astype(BF16)
-        each(m, l, ag_copy, "start")
+        each(layers, l, rs_layer, "wait_recv")
+        total = mid[l, layer].astype(F32)
+        for k in range(1, layers):
+            total = total + rsl[l, lax.rem(layer + k, layers)].astype(F32)
+        ag[l, core, place, layer] = total.astype(BF16)
+        each(layers, l, ag_layer, "start")
+
+    def spread(l):
+        each(layers, l, ag_layer, "wait_recv")
+        each(plane, l, ag_plane, "start")
+
+    def forward(l):
+        each(plane, l, ag_plane, "wait_recv")
+        fwd_copy(l).start()
 
     slot_back(0, cot)
     arr[0, me] = jnp.zeros_like(arr[0, me])
@@ -231,25 +276,30 @@
     def emit_one(rows, value):
         fg_out[rows, :] = value
 
+    reduce_middle(0)
     finish(1, wn1, emit_one)
     gradient(1, 1, feats, low, rest)
     sib_copy(1).start()
     reduce_end(0)
     reduce_start(1)
+    spread(0)
+    reduce_middle(1)
+    forward(0)
     reduce_end(1)
-    each(m, 0, ag_copy, "wait_recv")
-    fwd_copy(0).start()
-    each(m, 1, ag_copy, "wait_recv")
-    fwd_copy(1).start()
+    spread(1)
+    forward(1)
     each(n, 0, a2a_copy, "wait_send")
     each(n, 1, a2a_copy, "wait_send")
     for l in range(2):
         sib_copy(l).wait_send()
-        each(m, l, rs_copy, "wait_send")
-        each(m, l, ag_copy, "wait_send")
-    for l in range(2):
+        each(plane, l, rs_plane, "wait_send")
+        each(layers, l, rs_layer, "wait_send")
+        each(layers, l, ag_layer, "wait_send")
+        each(plane, l, ag_plane, "wait_send")
+    for l, outs in ((0, (gs2_out, gn2_out)), (1, (gs1_out, gn1_out))):
         fwd_copy(l).wait()
-        gr_out[l] = ag[l].reshape(gr_out.shape[1:])
+        for which, out in enumerate(outs):
+            out[...] = ag[l, which].reshape(out.shape)
 
 
 def per_device(
@@ -290,16 +340,18 @@
 
     live = jnp.arange(cap)[None, :] < send_count[0][:, None]
     idx = jnp.where(live, send_rows[0], -1).reshape(1, slots)
+    plane = 4
+    layers = m // plane
     chunk = f // m
     dma = pltpu.SemaphoreType.DMA
-    feat_grad, grads = pl.pallas_call(
+    feat_grad, *grads = pl.pallas_call(
         functools.partial(main_kernel, n),
         out_shape=(
             jax.ShapeDtypeStruct((nl, f), F32),
-            jax.ShapeDtypeStruct((2, 2, f, f), BF16),
-        ),
+        )
+        + (jax.ShapeDtypeStruct((f, f), BF16),) * 4,
         in_specs=[vmem] * 10,
-        out_specs=(vmem, vmem),
+        out_specs=(vmem,) * 5,
         scratch_shapes=[
             pltpu.VMEM((nl, f), BF16),
             pltpu.VMEM((nl, f), BF16),
@@ -312,17 +364,23 @@
             pltpu.VMEM((2, n, 2 * cap, f // 2), BF16),
             pltpu.VMEM((2, 2, f, f), F32),
             pltpu.VMEM((2, f, f), F32),
-            pltpu.VMEM((2, m, chunk, f), BF16),
-            pltpu.VMEM((2, m, chunk, f), BF16),
-            pltpu.VMEM((2, 2, m, chunk, f), BF16),
+            pltpu.VMEM((2, plane, layers, chunk, f), BF16),
+            pltpu.VMEM((2, plane, layers, chunk, f), BF16),
+            pltpu.VMEM((2, layers, chunk, f), BF16),
+            pltpu.VMEM((2, layers, chunk, f), BF16),
+            pltpu.VMEM((2, 2, plane, layers, chunk, f), BF16),
             dma((2, n)),
             dma((2, n)),
             dma((4,)),
             dma((4,)),
-            dma((2, m)),
-            dma((2, m)),
-            dma((2, m)),
-            dma((2, m)),
+            dma((2, plane)),
+            dma((2, plane)),
+            dma((2, layers)),
+            dma((2, layers)),
+            dma((2, layers)),
+            dma((2, layers)),
+            dma((2, plane)),
+            dma((2, plane)),
         ],
         compiler_params=pltpu.CompilerParams(
             collective_id=0, has_side_effects=True, vmem_limit_bytes=VMEM_LIMIT
@@ -340,8 +398,7 @@
         rt,
         idx,
     )
-    grads = grads.astype(F32)
-    return (feat_grad, grads[1, 0], grads[1, 1], grads[0, 0], grads[0, 1])
+    return (feat_grad, *(grad.astype(F32) for grad in grads))
 
 
 def solution(mesh):

time: 108 us -> 90.3 us (0.84)
  the two profiles are of different devices: /device:TPU:17 before, /device:TPU:0 now
where the time goes in v1:
time: 90.3 us; the launch traced here: 90.1 us
  Pallas kernels  77.7 us (86%)
  local copies, waits for them, and re-layouts  6.51 us (7%)
  other arithmetic  5.13 us (6%)
    pallas_call x1, Pallas kernels, per_device(): pl.pallas_call(functools.partial(main_kernel, n), out_shape=(jax.ShapeDty...  69.6 us
    pallas_call x1, Pallas kernels, per_device(): pl.pallas_call(dense_kernel, out_shape=(jax.ShapeDtypeStruct((2, nl, nl),...  8.17 us
    unnamed x15, local copies, waits for them, and re-layouts  6.33 us
    convert_element_type x4, other arithmetic, per_device(): return (feat_grad, *(grad.astype(F32) for grad in grads))  4.39 us

profile of v1, /device:TPU:0, one launch (start us, length us, event | category | flops | bytes accessed | tf_op | source)
XLA Modules:
  0.0 90.1 jit_solution(72398778491231458)
XLA Ops:
  0.6 0.7 iota_compare_fusion
  1.4 0.1 lt.29
  1.5 0.8 copy.21.coords
  2.2 0.8 copy.22
  3.0 0.1 squeeze.3
  3.1 0.0 copy-start
  3.1 1.1 %copy-done = bf16[24,128,128]{2,1,0:T(8,128)(2,1)S(1)} copy-done((bf16[24,128,128]{2,1,0:T(8,128)(2,1)S(1)}, bf16[24,128,128]{2,1,0:T(8,128)(2,1)}, u32[]{:S(2)}) %copy-start) | copy-done | bytes 786456
  4.2 0.0 copy-start.1
  4.2 1.0 %copy-done.1 = bf16[16,128,128]{2,1,0:T(8,128)(2,1)S(1)} copy-done((bf16[16,128,128]{2,1,0:T(8,128)(2,1)S(1)}, bf16[16,128,128]{2,1,0:T(8,128)(2,1)}, u32[]{:S(2)}) %copy-start.1) | copy-done | bytes 524312
  5.3 0.0 copy-start.2
  5.3 0.7 copy-done.2
  5.9 0.0 copy-start.3
  5.9 0.7 copy-done.3
  6.6 8.2 %dense.1 = (bf16[2,1024,1024]{2,1,0:T(8,128)(2,1)}, bf16[2,256,1024]{2,1,0:T(8,128)(2,1)}) custom-call(s32[24,2]{1,0:T(8,128)S(1)} %copy.21.coords, s32[16]{0:T(128)S(1)} %copy-done.2, s32[16]{0:T(128)S(1)} %copy-done.3, bf16[24,128,128]{2,1,0:T(8,128)(2,1)S(1)} %copy-done, bf16[16,128,128]{2,1,0:T(8,128)(2,1)S(1)} %copy-done.1), custom_call_target="tpu_custom_call" | custom-call | tf_op jit(solution)/shard_map/dense/pallas_call | solution.py:328
  14.7 69.6 %main.1 = (f32[1024,512]{1,0:T(8,128)}, bf16[512,512]{1,0:T(8,128)(2,1)S(1)}, bf16[512,512]{1,0:T(8,128)(2,1)S(1)}, bf16[512,512]{1,0:T(8,128)(2,1)S(1)}, bf16[512,512]{1,0:T(8,128)(2,1)}) custom-call(bf16[1024,512]{1,0:T(8,128)(2,1)} %feats.1, bf16[1024,512]{1,0:T(8,128)(2,1)} %pre.1, bf16[1024,512]{1,0:T(8,128)(2,1)} %cot.1, bf16[512,512]{1,0:T(8,128)(2,1)} %ws1.1, ...), custom_call_target="tpu_custom_call" | custom-call | tf_op jit(solution)/shard_map/main/pallas_call | solution.py:347
  84.3 0.0 copy-start.5
  84.3 1.1 %convert_element_type.12 = f32[512,512]{1,0:T(8,128)} convert(bf16[512,512]{1,0:T(8,128)(2,1)S(1)} %get-tuple-element.15) | non-fusion elementwise | flops 262144 | bytes 1572864 | tf_op jit(solution)/shard_map/convert_element_type | solution.py:401
  85.4 0.0 copy-start.4
  85.4 1.1 %convert_element_type.13 = f32[512,512]{1,0:T(8,128)} convert(bf16[512,512]{1,0:T(8,128)(2,1)S(1)} %get-tuple-element.16) | non-fusion elementwise | flops 262144 | bytes 1572864 | tf_op jit(solution)/shard_map/convert_element_type | solution.py:401
  86.5 1.1 %convert_element_type.14 = f32[512,512]{1,0:T(8,128)} convert(bf16[512,512]{1,0:T(8,128)(2,1)S(1)} %get-tuple-element.17) | non-fusion elementwise | flops 262144 | bytes 1572864 | tf_op jit(solution)/shard_map/convert_element_type | solution.py:401
  87.6 0.0 copy-done.5
  87.6 1.1 %convert_element_type.15 = f32[512,512]{1,0:T(8,128)} convert(bf16[512,512]{1,0:T(8,128)(2,1)S(1)} %copy-done.5) | non-fusion elementwise | flops 262144 | bytes 1572864 | tf_op jit(solution)/shard_map/convert_element_type | solution.py:401
  88.7 0.0 copy-done.4
  88.7 1.3 %copy.24 = f32[1024,512]{1,0:T(8,128)} copy(f32[1024,512]{1,0:T(8,128)S(1)} %copy-done.4) | data formatting | bytes 4194304
  (1 shorter events, 0.0 us)
Async XLA Ops:
  3.1 1.1 %copy-start = (bf16[24,128,128]{2,1,0:T(8,128)(2,1)S(1)}, bf16[24,128,128]{2,1,0:T(8,128)(2,1)}, u32[]{:S(2)}) copy-start(bf16[24,128,128]{2,1,0:T(8,128)(2,1)} %ltiles.1) | copy-start | bytes 2359300
  4.2 1.0 %copy-start.1 = (bf16[16,128,128]{2,1,0:T(8,128)(2,1)S(1)}, bf16[16,128,128]{2,1,0:T(8,128)(2,1)}, u32[]{:S(2)}) copy-start(bf16[16,128,128]{2,1,0:T(8,128)(2,1)} %rtiles.1) | copy-start | bytes 1572868
  5.3 0.7 copy-start.2
  5.9 0.7 copy-start.3
  84.3 3.3 %copy-start.5 = (bf16[512,512]{1,0:T(8,128)(2,1)S(1)}, bf16[512,512]{1,0:T(8,128)(2,1)}, u32[]{:S(2)}) copy-start(bf16[512,512]{1,0:T(8,128)(2,1)} %get-tuple-element.18) | copy-start | bytes 1572868
  85.4 3.3 %copy-start.4 = (f32[1024,512]{1,0:T(8,128)S(1)}, f32[1024,512]{1,0:T(8,128)}, u32[]{:S(2)}) copy-start(f32[1024,512]{1,0:T(8,128)} %get-tuple-element.24) | copy-start | bytes 6291460

commit v2 on v1

--- a/solution.py
+++ b/solution.py
@@ -22,13 +22,13 @@
     d_acc[...] = jnp.zeros_like(d_acc)
     rt_acc[...] = jnp.zeros_like(rt_acc)
 
-    @pl.loop(0, ltiles.shape[0])
+    @pl.loop(0, ltiles.shape[0], unroll=4)
     def _(t):
         r = pl.multiple_of(coords[t, 0] * side, side)
         q = pl.multiple_of(coords[t, 1] * side, side)
         d_acc[pl.ds(q, side), pl.ds(r, side)] += ltiles[t].astype(F32).T
 
-    @pl.loop(0, rtiles.shape[0])
+    @pl.loop(0, rtiles.shape[0], unroll=4)
     def _(t):
         r = pl.multiple_of(rrows[t] * side, side)
         q = pl.multiple_of(rslots[t] * side, side)

time: 90.3 us -> 87.7 us (0.971)
  Pallas kernels: 77.7 us -> 75.1 us
    pallas_call x1, Pallas kernels: 8.17 us -> 5.52 us  [per_device(): pl.pallas_call(dense_kernel, out_shape=(jax.ShapeDtypeStruct((2, nl, nl),...]
where the time goes in v2:
time: 87.7 us; the launch traced here: 87.4 us
  Pallas kernels  75.1 us (86%)
  local copies, waits for them, and re-layouts  6.51 us (7%)
  other arithmetic  5.13 us (6%)
    pallas_call x1, Pallas kernels, per_device(): pl.pallas_call(functools.partial(main_kernel, n), out_shape=(jax.ShapeDty...  69.6 us
    unnamed x15, local copies, waits for them, and re-layouts  6.33 us
    pallas_call x1, Pallas kernels, per_device(): pl.pallas_call(dense_kernel, out_shape=(jax.ShapeDtypeStruct((2, nl, nl),...  5.52 us
    convert_element_type x4, other arithmetic, per_device(): return (feat_grad, *(grad.astype(F32) for grad in grads))  4.39 us

profile of v2, /device:TPU:0, one launch (start us, length us, event | category | flops | bytes accessed | tf_op | source)
XLA Modules:
  0.0 87.4 jit_solution(6821539591291975660)
XLA Ops:
  0.6 0.7 iota_compare_fusion
  1.4 0.1 lt.29
  1.5 0.8 copy.21.coords
  2.2 0.8 copy.22
  3.0 0.1 squeeze.3
  3.1 0.0 copy-start
  3.1 1.1 %copy-done = bf16[24,128,128]{2,1,0:T(8,128)(2,1)S(1)} copy-done((bf16[24,128,128]{2,1,0:T(8,128)(2,1)S(1)}, bf16[24,128,128]{2,1,0:T(8,128)(2,1)}, u32[]{:S(2)}) %copy-start) | copy-done | bytes 786456
  4.2 0.0 copy-start.1
  4.2 1.0 %copy-done.1 = bf16[16,128,128]{2,1,0:T(8,128)(2,1)S(1)} copy-done((bf16[16,128,128]{2,1,0:T(8,128)(2,1)S(1)}, bf16[16,128,128]{2,1,0:T(8,128)(2,1)}, u32[]{:S(2)}) %copy-start.1) | copy-done | bytes 524312
  5.3 0.0 copy-start.2
  5.3 0.7 copy-done.2
  5.9 0.0 copy-start.3
  5.9 0.7 copy-done.3
  6.6 5.5 %dense.1 = (bf16[2,1024,1024]{2,1,0:T(8,128)(2,1)}, bf16[2,256,1024]{2,1,0:T(8,128)(2,1)}) custom-call(s32[24,2]{1,0:T(8,128)S(1)} %copy.21.coords, s32[16]{0:T(128)S(1)} %copy-done.2, s32[16]{0:T(128)S(1)} %copy-done.3, bf16[24,128,128]{2,1,0:T(8,128)(2,1)S(1)} %copy-done, bf16[16,128,128]{2,1,0:T(8,128)(2,1)S(1)} %copy-done.1), custom_call_target="tpu_custom_call" | custom-call | tf_op jit(solution)/shard_map/dense/pallas_call | solution.py:328
  12.1 69.6 %main.1 = (f32[1024,512]{1,0:T(8,128)}, bf16[512,512]{1,0:T(8,128)(2,1)S(1)}, bf16[512,512]{1,0:T(8,128)(2,1)S(1)}, bf16[512,512]{1,0:T(8,128)(2,1)S(1)}, bf16[512,512]{1,0:T(8,128)(2,1)}) custom-call(bf16[1024,512]{1,0:T(8,128)(2,1)} %feats.1, bf16[1024,512]{1,0:T(8,128)(2,1)} %pre.1, bf16[1024,512]{1,0:T(8,128)(2,1)} %cot.1, bf16[512,512]{1,0:T(8,128)(2,1)} %ws1.1, ...), custom_call_target="tpu_custom_call" | custom-call | tf_op jit(solution)/shard_map/main/pallas_call | solution.py:347
  81.7 0.0 copy-start.5
  81.7 1.1 %convert_element_type.12 = f32[512,512]{1,0:T(8,128)} convert(bf16[512,512]{1,0:T(8,128)(2,1)S(1)} %get-tuple-element.15) | non-fusion elementwise | flops 262144 | bytes 1572864 | tf_op jit(solution)/shard_map/convert_element_type | solution.py:401
  82.8 0.0 copy-start.4
  82.8 1.1 %convert_element_type.13 = f32[512,512]{1,0:T(8,128)} convert(bf16[512,512]{1,0:T(8,128)(2,1)S(1)} %get-tuple-element.16) | non-fusion elementwise | flops 262144 | bytes 1572864 | tf_op jit(solution)/shard_map/convert_element_type | solution.py:401
  83.9 1.1 %convert_element_type.14 = f32[512,512]{1,0:T(8,128)} convert(bf16[512,512]{1,0:T(8,128)(2,1)S(1)} %get-tuple-element.17) | non-fusion elementwise | flops 262144 | bytes 1572864 | tf_op jit(solution)/shard_map/convert_element_type | solution.py:401
  85.0 0.0 copy-done.5
  85.0 1.1 %convert_element_type.15 = f32[512,512]{1,0:T(8,128)} convert(bf16[512,512]{1,0:T(8,128)(2,1)S(1)} %copy-done.5) | non-fusion elementwise | flops 262144 | bytes 1572864 | tf_op jit(solution)/shard_map/convert_element_type | solution.py:401
  86.1 0.0 copy-done.4
  86.1 1.3 %copy.24 = f32[1024,512]{1,0:T(8,128)} copy(f32[1024,512]{1,0:T(8,128)S(1)} %copy-done.4) | data formatting | bytes 4194304
  (1 shorter events, 0.0 us)
Async XLA Ops:
  3.1 1.1 %copy-start = (bf16[24,128,128]{2,1,0:T(8,128)(2,1)S(1)}, bf16[24,128,128]{2,1,0:T(8,128)(2,1)}, u32[]{:S(2)}) copy-start(bf16[24,128,128]{2,1,0:T(8,128)(2,1)} %ltiles.1) | copy-start | bytes 2359300
  4.2 1.0 %copy-start.1 = (bf16[16,128,128]{2,1,0:T(8,128)(2,1)S(1)}, bf16[16,128,128]{2,1,0:T(8,128)(2,1)}, u32[]{:S(2)}) copy-start(bf16[16,128,128]{2,1,0:T(8,128)(2,1)} %rtiles.1) | copy-start | bytes 1572868
  5.3 0.7 copy-start.2
  5.9 0.7 copy-start.3
  81.7 3.3 %copy-start.5 = (bf16[512,512]{1,0:T(8,128)(2,1)S(1)}, bf16[512,512]{1,0:T(8,128)(2,1)}, u32[]{:S(2)}) copy-start(bf16[512,512]{1,0:T(8,128)(2,1)} %get-tuple-element.18) | copy-start | bytes 1572868
  82.8 3.3 %copy-start.4 = (f32[1024,512]{1,0:T(8,128)S(1)}, f32[1024,512]{1,0:T(8,128)}, u32[]{:S(2)}) copy-start(f32[1024,512]{1,0:T(8,128)} %get-tuple-element.24) | copy-start | bytes 6291460
